TPU v7x, 32 devices: a whole 2x2x4 slice. The times are simulated.
32 devices in a mesh: groups: 2 (over y), obs: 4 (over z), cam: 4 (over x, core).
Axes of the slice: x: 2, y: 2, z: 4, core: 2. Of those that a mesh axis runs over, the one named last changes fastest.
Arguments:
- cameras: float32 [9, 1024], P(None, ('groups', 'cam')), parts along dimension 1, may hold values from -1 to 6, as said below
- points: float32 [3, 2048], P(None, ('groups', 'obs')), parts along dimension 1, may hold values from -1 to 1
- measured: float32 [256, 2, 128], P(('groups', 'obs', 'cam')), parts along dimension 0, may hold values from -1.5 to 1.5
- sqrt_weight: float32 [256, 128], P(('groups', 'obs', 'cam')), parts along dimension 0, may hold values from 0.5 to 2
- cam_index: int32 [256, 128], P(('groups', 'obs', 'cam')), parts along dimension 0, may hold values from 0 to 511
- point_slot: int32 [256, 128], P(('groups', 'obs', 'cam')), parts along dimension 0, may hold values from 0 to 255
- block_owner: int32 [256, 1], P(('groups', 'obs', 'cam')), parts along dimension 0, may hold values from 0 to 3; in each aligned block of 8 rows (0 to 7, 8 to 15, ...) at most 4 rows name the same one
- valid_count: int32 [256], P(('groups', 'obs', 'cam')), parts along dimension 0, may hold values from 32 to 128
Outputs:
- camera_step: float32 [9, 1024], P(None, ('groups', 'cam')), parts along dimension 1
- point_step: float32 [3, 2048], P(None, ('groups', 'obs')), parts along dimension 1
There are 2 independent parts, one for each index of `groups`. A program takes and returns all parts, laid end to end along the dimension named above; each array names one. Nothing has to cross between parts.
Inputs may be any that keep to these rules, and one draw needn't show every extreme that they name: `cameras`: rows 0 to 2 lie in [-0.3, 0.3], rows 3 and 4 in [-1, 1], row 5 in [4, 6], row 6 in [0.5, 2], row 7 in [-0.2, 0.2], row 8 in [-0.1, 0.1]. `block_owner`: among the 8 rows of one device no shard is named by more than 4 rows, a bound that some block reaches.
All inputs are finite; a program needn't handle non-finite values.
Results may differ from a plain program's by a relative error of at most 0.0003.
Values sent between devices are 32-bit elements; how exact they have to be, the bound alone decides.
A program may use at most 64 MiB of HBM per device.

v0:
```python
import jax
import jax.numpy as jnp
from jax import lax
from jax.sharding import PartitionSpec as P

ITERS = 3


damping = 0.1
PAIR_LIST = ((9, 9), (9, 10), (9, 11), (10, 10), (10, 11), (11, 11))


def project(
    rot_a,
    rot_b,
    rot_c,
    move_a,
    move_b,
    move_c,
    focal_len,
    radial_a,
    radial_b,
    land_a,
    land_b,
    land_c,
):
    angle_sq = rot_a * rot_a + rot_b * rot_b + rot_c * rot_c
    first_coef = 1.0 - angle_sq / 6.0 + angle_sq * angle_sq / 120.0
    second_coef = 0.5 - angle_sq / 24.0 + angle_sq * angle_sq / 720.0
    cross_a = rot_b * land_c - rot_c * land_b
    cross_b = rot_c * land_a - rot_a * land_c
    cross_c = rot_a * land_b - rot_b * land_a
    twice_a = rot_b * cross_c - rot_c * cross_b
    twice_b = rot_c * cross_a - rot_a * cross_c
    twice_c = rot_a * cross_b - rot_b * cross_a
    frame_a = land_a + first_coef * cross_a + second_coef * twice_a + move_a
    frame_b = land_b + first_coef * cross_b + second_coef * twice_b + move_b
    frame_c = land_c + first_coef * cross_c + second_coef * twice_c + move_c
    plane_u = frame_a / frame_c
    plane_v = frame_b / frame_c
    radius_sq = plane_u * plane_u + plane_v * plane_v
    stretch = focal_len * (1.0 + radial_a * radius_sq + radial_b * radius_sq * radius_sq)
    return (stretch * plane_u, stretch * plane_v)


def linearize_residuals(model_parameters, measurement_u, measurement_v, robust_weighting):
    primals = tuple(model_parameters)
    entry_values, pullback = jax.vjp(project, *primals)
    all_ones = jnp.ones_like(entry_values[0])
    all_zeros = jnp.zeros_like(entry_values[0])
    grads_u = pullback((all_ones, all_zeros))
    grads_v = pullback((all_zeros, all_ones))
    slopes_u = [robust_weighting * member for member in grads_u]
    slopes_v = [robust_weighting * member for member in grads_v]
    residual_u = robust_weighting * (entry_values[0] - measurement_u)
    residual_v = robust_weighting * (entry_values[1] - measurement_v)
    return (residual_u, residual_v, slopes_u, slopes_v)


def solve_three(upper, right):
    minor_aa = upper[3] * upper[5] - upper[4] * upper[4]
    minor_ab = upper[2] * upper[4] - upper[1] * upper[5]
    minor_ac = upper[1] * upper[4] - upper[2] * upper[3]
    minor_bb = upper[0] * upper[5] - upper[2] * upper[2]
    minor_bc = upper[1] * upper[2] - upper[0] * upper[4]
    minor_cc = upper[0] * upper[3] - upper[1] * upper[1]
    determinant = upper[0] * minor_aa + upper[1] * minor_ab + upper[2] * minor_ac
    return (
        (minor_aa * right[0] + minor_ab * right[1] + minor_ac * right[2]) / determinant,
        (minor_ab * right[0] + minor_bb * right[1] + minor_bc * right[2]) / determinant,
        (minor_ac * right[0] + minor_bc * right[1] + minor_cc * right[2]) / determinant,
    )


def across_cams(partials):
    return lax.psum(tuple(partials), "cam")


def local(cameras, points, measured, sqrt_weight, cam_index, point_slot, block_owner, valid_count):
    obs_count = lax.axis_size("obs")
    cam_count = lax.axis_size("cam")
    blocks, block_len = cam_index.shape
    pts_local = points.shape[1]
    cams_local = cameras.shape[1]
    cams_all = cams_local * cam_count
    owner_ids = block_owner[:, 0]
    lane_ids = lax.broadcasted_iota(jnp.int32, (blocks, block_len), 1)
    in_use = (lane_ids < valid_count[:, None]).astype(jnp.float32)
    robust_weighting = sqrt_weight * in_use
    flat_cam = cam_index.reshape(-1)
    own_points = (points[0], points[1], points[2])
    global_ids = (owner_ids[:, None] * pts_local + point_slot).reshape(-1)
    pts_all = pts_local * obs_count

    def point_sum(summands):
        spread = tuple(
            (
                jnp.zeros((pts_all,), jnp.float32).at[global_ids].add(summand.reshape(-1))
                for summand in summands
            )
        )
        return across_cams(lax.psum_scatter(spread, "obs", scatter_dimension=0, tiled=True))

    def at_points(point_values):
        gathered = lax.all_gather(tuple(point_values), "obs", axis=0, tiled=True)
        return tuple((received[global_ids].reshape(blocks, block_len) for received in gathered))

    def camera_sum(summands):
        spread = tuple(
            (
                jnp.zeros((cams_all,), jnp.float32).at[flat_cam].add(summand.reshape(-1))
                for summand in summands
            )
        )
        shares = lax.psum_scatter(spread, "cam", scatter_dimension=0, tiled=True)
        return lax.psum(shares, "obs")

    def camera_dot(left_vec, right_vec):
        return lax.psum(jnp.sum(left_vec * right_vec), "cam")

    all_cams = lax.all_gather(cameras, "cam", axis=1, tiled=True)
    positions = at_points(own_points)
    model_parameters = [all_cams[member][cam_index] for member in range(9)] + list(positions)
    residual_u, residual_v, slopes_u, slopes_v = linearize_residuals(
        model_parameters, measured[:, 0, :], measured[:, 1, :], robust_weighting
    )
    setup_rows = [
        slopes_u[first_pos] * slopes_u[second_pos] + slopes_v[first_pos] * slopes_v[second_pos]
        for first_pos, second_pos in PAIR_LIST
    ]
    setup_rows += [
        slopes_u[9 + member] * residual_u + slopes_v[9 + member] * residual_v for member in range(3)
    ]
    totals = point_sum(setup_rows)
    normal = tuple(
        (totals[member] + damping if member in (0, 3, 5) else totals[member] for member in range(6))
    )
    gradient_pts = totals[6:]
    shifted = at_points(solve_three(normal, gradient_pts))
    back_u = sum((slopes_u[9 + member] * shifted[member] for member in range(3)))
    back_v = sum((slopes_v[9 + member] * shifted[member] for member in range(3)))
    cam_rows = [
        -(slopes_u[member] * residual_u + slopes_v[member] * residual_v)
        + slopes_u[member] * back_u
        + slopes_v[member] * back_v
        for member in range(9)
    ]
    cam_rows += [
        slopes_u[member] * slopes_u[member] + slopes_v[member] * slopes_v[member]
        for member in range(9)
    ]
    cam_totals = camera_sum(cam_rows)
    rhs = jnp.stack(cam_totals[:9])
    precond = jnp.stack(cam_totals[9:]) + damping

    def along_cameras(direction):
        full_dir = lax.all_gather(direction, "cam", axis=1, tiled=True)
        at_obs = [full_dir[member][cam_index] for member in range(9)]
        along_u = sum((slopes_u[member] * at_obs[member] for member in range(9)))
        along_v = sum((slopes_v[member] * at_obs[member] for member in range(9)))
        return (along_u, along_v)

    def apply_schur(direction):
        along_u, along_v = along_cameras(direction)
        pushed = point_sum(
            [slopes_u[9 + member] * along_u + slopes_v[9 + member] * along_v for member in range(3)]
        )
        pulled = at_points(solve_three(normal, pushed))
        left_u = along_u - sum((slopes_u[9 + member] * pulled[member] for member in range(3)))
        left_v = along_v - sum((slopes_v[9 + member] * pulled[member] for member in range(3)))
        summed = camera_sum(
            [slopes_u[member] * left_u + slopes_v[member] * left_v for member in range(9)]
        )
        return jnp.stack(summed) + damping * direction

    solution = jnp.zeros_like(rhs)
    residual = rhs
    scaled_res = residual / precond
    search = scaled_res
    inner = camera_dot(residual, scaled_res)
    for step in range(ITERS):
        image = apply_schur(search)
        step_len = inner / camera_dot(search, image)
        solution = solution + step_len * search
        residual = residual - step_len * image
        if step + 1 < ITERS:
            scaled_res = residual / precond
            inner_next = camera_dot(residual, scaled_res)
            search = scaled_res + inner_next / inner * search
            inner = inner_next
    along_u, along_v = along_cameras(solution)
    pushed = point_sum(
        [slopes_u[9 + member] * along_u + slopes_v[9 + member] * along_v for member in range(3)]
    )
    update = solve_three(normal, [-(gradient_pts[member] + pushed[member]) for member in range(3)])
    return (solution, jnp.stack(update))


def solution(mesh):
    return jax.shard_map(
        local,
        mesh=mesh,
        in_specs=(
            P(None, ("groups", "cam")),
            P(None, ("groups", "obs")),
            P(("groups", "obs", "cam"), None, None),
            P(("groups", "obs", "cam"), None),
            P(("groups", "obs", "cam"), None),
            P(("groups", "obs", "cam"), None),
            P(("groups", "obs", "cam"), None),
            P(("groups", "obs", "cam")),
        ),
        out_specs=(P(None, ("groups", "cam")), P(None, ("groups", "obs"))),
        check_vma=False,
    )
```

profile of v0, /device:TPU:0, one launch (start us, length us, event | category | flops | bytes accessed | tf_op | source)
XLA Modules:
  0.0 1285.2 jit_solution(1156818286051668134)
XLA Ops:
  3.9 12.6 all-gather
  33.9 9.6 all-gather.1
  254.4 16.1 %all-reduce.84 = (f32[1024]{0:T(1024)S(1)}, f32[1024]{0:T(1024)S(1)}, f32[1024]{0:T(1024)S(1)}, f32[1024]{0:T(1024)S(1)}, f32[1024]{0:T(1024)S(1)}, /*index=5*/f...) all-reduce(f32[1024]{0:T(1024)S(1)} %scatter_custom_fusion.4, ...), channel_id=9, replica_groups=mesh['groups'=2,'obs'=4,'cam'=4] {'obs'}, use_global_device_ids=true, to_apply=%region_13.0.clone | all-reduce | flops 9216 | bytes 73728
  277.0 9.5 all-gather.5
  303.2 9.5 all-gather.3
  340.2 8.0 scatter_custom_fusion.15
  386.3 10.5 all-reduce.74
  397.5 8.8 all-reduce.83
  496.5 17.3 %all-reduce.82 = (f32[1024]{0:T(1024)S(1)}, f32[1024]{0:T(1024)S(1)}, f32[1024]{0:T(1024)S(1)}) all-reduce(f32[1024]{0:T(1024)S(1)} %scatter_custom_fusion.29, f32[1024]{0:T(1024)S(1)} %scatter_custom_fusion.28, f32[1024]{0:T(1024)S(1)} %scatter_custom_fusion.27), channel_id=34, replica_groups=mesh['groups'=2,'obs'=4,'cam'=4] {'obs'}, use_global_device_ids=true, to_apply=%region_90.0.clone | all-reduce | flops 3072 | bytes 24576
  531.8 9.6 all-gather.6
  626.8 10.2 all-reduce.72
  637.7 10.5 all-reduce.81
  756.2 15.9 %all-reduce.80 = (f32[1024]{0:T(1024)S(1)}, f32[1024]{0:T(1024)S(1)}, f32[1024]{0:T(1024)S(1)}) all-reduce(f32[1024]{0:T(1024)S(1)} %scatter_custom_fusion.41, f32[1024]{0:T(1024)S(1)} %scatter_custom_fusion.40, f32[1024]{0:T(1024)S(1)} %scatter_custom_fusion.39), channel_id=46, replica_groups=mesh['groups'=2,'obs'=4,'cam'=4] {'obs'}, use_global_device_ids=true, to_apply=%region_130.0.clone | all-reduce | flops 3072 | bytes 24576
  778.0 8.4 all-gather.11
  790.9 8.7 all-gather.9
  804.2 8.4 all-gather.10
  885.9 10.6 all-reduce.69
  897.2 9.7 all-reduce.79
  1013.6 16.2 %all-reduce.78 = (f32[1024]{0:T(1024)S(1)}, f32[1024]{0:T(1024)S(1)}, f32[1024]{0:T(1024)S(1)}) all-reduce(f32[1024]{0:T(1024)S(1)} %scatter_custom_fusion.53, f32[1024]{0:T(1024)S(1)} %scatter_custom_fusion.52, f32[1024]{0:T(1024)S(1)} %scatter_custom_fusion.51), channel_id=58, replica_groups=mesh['groups'=2,'obs'=4,'cam'=4] {'obs'}, use_global_device_ids=true, to_apply=%region_170.0.clone | all-reduce | flops 3072 | bytes 24576
  1047.9 9.4 all-gather.12
  1061.8 8.0 all-gather.13
  1143.0 10.2 all-reduce.67
  1153.9 10.3 all-reduce.77
  1262.7 15.6 %all-reduce.76 = (f32[1024]{0:T(1024)S(1)}, f32[1024]{0:T(1024)S(1)}, f32[1024]{0:T(1024)S(1)}) all-reduce(f32[1024]{0:T(1024)S(1)} %scatter_custom_fusion.63, f32[1024]{0:T(1024)S(1)} %scatter_custom_fusion.64, f32[1024]{0:T(1024)S(1)} %scatter_custom_fusion.65), channel_id=68, replica_groups=mesh['groups'=2,'obs'=4,'cam'=4] {'obs'}, use_global_device_ids=true, to_apply=%region_202.0.clone | all-reduce | flops 3072 | bytes 24576
  (285 shorter events, 1011.3 us)
Async XLA Ops:
  0.6 0.7 copy-start.10
  1.9 0.7 copy-start.9
  3.1 0.7 copy-start.6
  3.1 0.7 copy-start.8
  3.9 12.6 copy-start.5
  16.6 0.7 copy-start.1
  48.0 0.7 copy-start.3
  48.7 0.7 copy-start.2
  109.6 6.9 copy-start.4
  109.6 6.9 copy-start.7
  1172.4 5.5 copy-start
where the time goes:
time: 1290 us
  other arithmetic  508 us (39%)
  local copies, waits for them, and re-layouts  385 us (30%)
  blocking collectives  381 us (30%)
    scatter-add x45, other arithmetic, camera_sum(): jnp.zeros((cams_all,), jnp.float32).at[flat_cam].add(summand.reshape(-1))  344 us
    gather x36, local copies, waits for them, and re-layouts, along_cameras(): at_obs = [full_dir[member][cam_index] for member in range(9)]  247 us
    scatter-add x21, other arithmetic, point_sum(): jnp.zeros((pts_all,), jnp.float32).at[global_ids].add(summand.reshape(-1))  160 us
    all_gather x15, blocking collectives, at_points(): gathered = lax.all_gather(tuple(point_values), 'obs', axis=0, tiled=True)  132 us
    unnamed x9, blocking collectives  123 us
    gather x15, local copies, waits for them, and re-layouts, at_points(): received[global_ids].reshape(blocks, block_len)  67.8 us
    gather x9, local copies, waits for them, and re-layouts, local(): all_cams[member][cam_index]  61.8 us
    psum x4, blocking collectives, camera_sum(): return lax.psum(shares, 'obs')  39.2 us

commit v1 on v0

v1 whole, which is shorter than its diff:
```python
import functools

import jax
import jax.numpy as jnp
from jax import lax
from jax.experimental import pallas as pl
from jax.experimental.pallas import tpu as pltpu
from jax.sharding import PartitionSpec as P

ITERS = 3
DAMPING = 0.1
PAIR_LIST = ((0, 0), (0, 1), (0, 2), (1, 1), (1, 2), (2, 2))
F32, BF16 = jnp.float32, jnp.bfloat16


def ceil_to(number, step):
    return -(-number // step) * step


def cross(a, b):
    return (a[1] * b[2] - a[2] * b[1], a[2] * b[0] - a[0] * b[2], a[0] * b[1] - a[1] * b[0])


def inner3(a, b):
    return a[0] * b[0] + a[1] * b[1] + a[2] * b[2]


def linearize(cam, point):
    w, t = cam[0:3], cam[3:6]
    focal, k1, k2 = cam[6], cam[7], cam[8]
    s = inner3(w, w)
    a = 1.0 - s / 6.0 + s * s / 120.0
    c = 0.5 - s / 24.0 + s * s / 720.0
    a_slope = -1.0 / 6.0 + s / 60.0
    c_slope = -1.0 / 24.0 + s / 360.0
    once = cross(w, point)
    twice = cross(w, once)
    frame = [point[i] + a * once[i] + c * twice[i] + t[i] for i in range(3)]
    inv = 1.0 / frame[2]
    u, v = frame[0] * inv, frame[1] * inv
    rho = u * u + v * v
    bend = 1.0 + k1 * rho + k2 * rho * rho
    bend_slope = k1 + 2.0 * k2 * rho
    scale = focal * inv
    uu = scale * (bend + 2.0 * u * u * bend_slope)
    uv = scale * (2.0 * u * v * bend_slope)
    vv = scale * (bend + 2.0 * v * v * bend_slope)
    grads = []
    for flat, g in ((u, (uu, uv, -(uu * u + uv * v))), (v, (uv, vv, -(uv * u + vv * v)))):
        along = 2.0 * (a_slope * inner3(g, once) + c_slope * inner3(g, twice))
        first, second, third = cross(point, g), cross(once, g), cross(point, cross(g, w))
        rot = [along * w[i] + a * first[i] + c * (second[i] + third[i]) for i in range(3)]
        wg = cross(w, g)
        wwg = cross(w, wg)
        land = [g[i] - a * wg[i] + c * wwg[i] for i in range(3)]
        fu = focal * rho * flat
        grads.append(rot + list(g) + [bend * flat, fu, fu * rho] + land)
    return focal * bend * u, focal * bend * v, grads[0], grads[1]


def pieces(x):
    high = x.astype(BF16)
    rest = x - high.astype(F32)
    mid = rest.astype(BF16)
    low = (rest - mid.astype(F32)).astype(BF16)
    return jnp.concatenate([high, mid, low], axis=0)


def joined(out):
    rows = out.shape[0] // 3
    return out[:rows] + (out[rows : 2 * rows] + out[2 * rows :])


def pad_rows(x, step):
    rows = x.shape[0]
    full = ceil_to(rows, step)
    if full == rows:
        return x
    return jnp.concatenate([x, jnp.zeros((full - rows, x.shape[1]), x.dtype)], axis=0)


def kernel(
    n_obs, n_cam,
    cameras, points, measured, weights, cam_index, point_slot, owner, valid,
    cam_out, point_out,
    cams_in, pts_in, setup_c, setup_o, pre_c, pre_o, push_c, push_o, sum_c, sum_o,
    cam_hot, pt_hot, slopes_u, slopes_v, full_x, full_p,
    send, recv,
):
    blocks, width = cam_index.shape
    slots = blocks * width
    pts_local = points.shape[1]
    cams_local = cameras.shape[1]
    cams_all = cams_local * n_cam
    chunks = cams_all // 128
    one = ceil_to(9 * chunks, 8)
    me = {"obs": lax.axis_index("obs"), "cam": lax.axis_index("cam")}
    size = {"obs": n_obs, "cam": n_cam}

    def partner(axis, step):
        return {axis: lax.rem(me[axis] + step, size[axis])}

    barrier = pltpu.get_barrier_semaphore()
    for axis in ("cam", "obs"):
        for step in range(1, size[axis]):
            pl.semaphore_signal(
                barrier, inc=1, device_id=partner(axis, step), device_id_type=pl.DeviceIdType.MESH
            )
    pl.semaphore_wait(barrier, n_obs + n_cam - 2)

    def begin(buf, number, axis):
        copies = []
        for step in range(1, size[axis]):
            copy = pltpu.make_async_remote_copy(
                src_ref=buf.at[me[axis]],
                dst_ref=buf.at[me[axis]],
                send_sem=send.at[number, step],
                recv_sem=recv.at[number, step],
                device_id=partner(axis, step),
                device_id_type=pl.DeviceIdType.MESH,
            )
            copy.start()
            copies.append(copy)
        return copies

    def finish(copies):
        for copy in copies:
            copy.wait()

    def total(buf, count):
        out = buf[0]
        for i in range(1, count):
            out = out + buf[i]
        return out

    def all_sum(first, second, number):
        finish(begin(first, number, "cam"))
        second[me["obs"]] = total(first, n_cam)
        finish(begin(second, number + 1, "obs"))
        return total(second, n_obs)

    cams_in[me["cam"]] = pad_rows(cameras[...], 16)
    pts_in[me["obs"]] = pad_rows(points[...], 8)
    copies = begin(cams_in, 0, "cam") + begin(pts_in, 1, "obs")

    def line(rows):
        return jnp.concatenate(rows, axis=1)

    cam_line = line([cam_index[b : b + 1, :] for b in range(blocks)])
    slot_line = line([point_slot[b : b + 1, :] for b in range(blocks)])
    owner_line = line([jnp.full((1, width), owner[b, 0], jnp.int32) for b in range(blocks)])
    meas_u = line([measured[b, 0:1, :] for b in range(blocks)])
    meas_v = line([measured[b, 1:2, :] for b in range(blocks)])
    lanes = lax.broadcasted_iota(jnp.int32, (1, width), 1)
    weight = line(
        [jnp.where(lanes < valid[b], weights[b : b + 1, :], 0.0) for b in range(blocks)]
    )
    for hot, index in ((cam_hot, cam_line), (pt_hot, slot_line)):
        for base in range(0, hot.shape[0], 128):
            ids = lax.broadcasted_iota(jnp.int32, (128, slots), 0) + base
            hot[base : base + 128, :] = jnp.where(ids == index, 1.0, 0.0).astype(BF16)
    mask = jnp.where(lax.broadcasted_iota(jnp.int32, (n_obs, slots), 0) == owner_line, 1.0, 0.0)

    def gather(x, hot):
        return joined(jnp.dot(pieces(x), hot[...], preferred_element_type=F32))

    def scatter(x, hot):
        return joined(
            lax.dot_general(
                pieces(x), hot[...], (((1,), (1,)), ((), ())), preferred_element_type=F32
            )
        )

    def to_points(rows):
        spread = jnp.concatenate([row * mask for row in rows], axis=0)
        return scatter(pad_rows(spread, 16), pt_hot)

    def from_points(members):
        got = gather(pad_rows(jnp.concatenate(members, axis=0), 16), pt_hot)
        return [
            jnp.sum(got[i * n_obs : (i + 1) * n_obs] * mask, axis=0, keepdims=True)
            for i in range(len(members))
        ]

    def members_of(table, count):
        return [table[i * n_obs : (i + 1) * n_obs] for i in range(count)]

    def pack(buf, vectors):
        for q, x in enumerate(vectors):
            for j in range(chunks):
                at, part = q * one + 8 * j, slice(128 * j, 128 * j + 128)
                buf[me["cam"], at : at + 8, :] = x[0:8, part]
                at = q * one + 8 * chunks + j
                buf[me["cam"], at : at + 1, :] = x[8:9, part]

    def unpack(table, q):
        base = q * one
        top = line([table[base + 8 * j : base + 8 * j + 8] for j in range(chunks)])
        base = base + 8 * chunks
        last = line([table[base + j : base + j + 1] for j in range(chunks)])
        return jnp.concatenate([top, last, jnp.zeros((7, cams_all), F32)], axis=0)

    pre_c[me["cam"]] = jnp.zeros(pre_c.shape[1:], F32)
    sum_c[me["cam"]] = jnp.zeros(sum_c.shape[1:], F32)
    finish(copies)

    params = gather(line([cams_in[j] for j in range(n_cam)]), cam_hot)
    places = from_points(
        [jnp.concatenate([pts_in[o, r : r + 1, :] for o in range(n_obs)], axis=0) for r in range(3)]
    )
    proj_u, proj_v, grads_u, grads_v = linearize([params[i : i + 1] for i in range(9)], places)
    resid_u, resid_v = weight * (proj_u - meas_u), weight * (proj_v - meas_v)
    for slopes, grads in ((slopes_u, grads_u), (slopes_v, grads_v)):
        slopes[...] = jnp.zeros_like(slopes)
        for i in range(9):
            slopes[i : i + 1, :] = weight * grads[i]
    land_u = [weight * grads_u[9 + i] for i in range(3)]
    land_v = [weight * grads_v[9 + i] for i in range(3)]

    rows = [land_u[i] * land_u[j] + land_v[i] * land_v[j] for i, j in PAIR_LIST]
    rows += [land_u[i] * resid_u + land_v[i] * resid_v for i in range(3)]
    setup_c[me["cam"]] = to_points(rows)
    totals = members_of(all_sum(setup_c, setup_o, 2), 9)
    full = [totals[i] + DAMPING if i in (0, 3, 5) else totals[i] for i in range(6)]
    gradient = totals[6:]
    minors = (
        full[3] * full[5] - full[4] * full[4],
        full[2] * full[4] - full[1] * full[5],
        full[1] * full[4] - full[2] * full[3],
        full[0] * full[5] - full[2] * full[2],
        full[1] * full[2] - full[0] * full[4],
        full[0] * full[3] - full[1] * full[1],
    )
    det = full[0] * minors[0] + full[1] * minors[1] + full[2] * minors[2]
    inverse = [minor / det for minor in minors]

    def solve(right):
        picks = ((0, 1, 2), (1, 3, 4), (2, 4, 5))
        return [sum(inverse[p[i]] * right[i] for i in range(3)) for p in picks]

    def at_slots(values):
        pulled = from_points(values)
        return inner3(land_u, pulled), inner3(land_v, pulled)

    back_u, back_v = at_slots(solve(gradient))
    ju, jv = slopes_u[...], slopes_v[...]
    both = scatter(
        jnp.concatenate(
            [ju * (back_u - resid_u) + jv * (back_v - resid_v), ju * ju + jv * jv], axis=0
        ),
        cam_hot,
    )
    pack(pre_c, [both[:16], both[16:]])
    table = all_sum(pre_c, pre_o, 4)
    rhs = unpack(table, 0)
    precond = unpack(table, 1) + DAMPING

    def push(x):
        at_obs = gather(x, cam_hot)
        along_u = jnp.sum(slopes_u[...] * at_obs, axis=0, keepdims=True)
        along_v = jnp.sum(slopes_v[...] * at_obs, axis=0, keepdims=True)
        push_c[me["cam"]] = to_points([land_u[i] * along_u + land_v[i] * along_v for i in range(3)])
        return along_u, along_v, members_of(all_sum(push_c, push_o, 6), 3)

    def dot(a, b):
        return jnp.sum(jnp.sum(a * b, axis=0, keepdims=True), axis=1, keepdims=True)

    def iterate(_, state):
        x, res, direction, rz = state
        along_u, along_v, pushed = push(direction)
        pulled_u, pulled_v = at_slots(solve(pushed))
        left_u, left_v = along_u - pulled_u, along_v - pulled_v
        pack(sum_c, [scatter(slopes_u[...] * left_u + slopes_v[...] * left_v, cam_hot)])
        image = unpack(all_sum(sum_c, sum_o, 8), 0) + DAMPING * direction
        alpha = rz / dot(direction, image)
        x = x + alpha * direction
        res = res - alpha * image
        pre = res / precond
        rz_new = dot(res, pre)
        return x, res, pre + (rz_new / rz) * direction, rz_new

    pre = rhs / precond
    state = (jnp.zeros_like(rhs), rhs, pre, dot(rhs, pre))
    x = lax.fori_loop(0, ITERS, iterate, state)[0]
    full_x[...] = x
    at = pl.multiple_of(me["cam"] * cams_local, cams_local)
    cam_out[...] = full_x[0:9, pl.ds(at, cams_local)]
    pushed = push(x)[2]
    steps = solve([-(gradient[i] + pushed[i]) for i in range(3)])
    for i in range(3):
        full_p[i] = steps[i]
        point_out[i : i + 1, :] = full_p[i, pl.ds(me["obs"], 1), :]


def local(cameras, points, measured, sqrt_weight, cam_index, point_slot, block_owner, valid_count):
    n_obs, n_cam = lax.axis_size("obs"), lax.axis_size("cam")
    slots = cam_index.shape[0] * cam_index.shape[1]
    pts_local, cams_local = points.shape[1], cameras.shape[1]
    cams_all = cams_local * n_cam
    one = ceil_to(9 * (cams_all // 128), 8)
    three, nine = ceil_to(3 * n_obs, 16), ceil_to(9 * n_obs, 16)

    def pair(rows, columns):
        return [pltpu.VMEM((count, rows, columns), F32) for count in (n_cam, n_obs)]

    vmem, smem = pl.BlockSpec(memory_space=pltpu.VMEM), pl.BlockSpec(memory_space=pltpu.SMEM)
    return pl.pallas_call(
        functools.partial(kernel, n_obs, n_cam),
        out_shape=(
            jax.ShapeDtypeStruct((9, cams_local), F32),
            jax.ShapeDtypeStruct((3, pts_local), F32),
        ),
        in_specs=[vmem] * 6 + [smem] * 2,
        out_specs=(vmem, vmem),
        scratch_shapes=[
            pltpu.VMEM((n_cam, 16, cams_local), F32),
            pltpu.VMEM((n_obs, 8, pts_local), F32),
            *pair(nine, pts_local),
            *pair(2 * one, 128),
            *pair(three, pts_local),
            *pair(one, 128),
            pltpu.VMEM((cams_all, slots), BF16),
            pltpu.VMEM((pts_local, slots), BF16),
            pltpu.VMEM((16, slots), F32),
            pltpu.VMEM((16, slots), F32),
            pltpu.VMEM((16, cams_all), F32),
            pltpu.VMEM((3, n_obs, pts_local), F32),
            pltpu.SemaphoreType.DMA((10, max(n_obs, n_cam))),
            pltpu.SemaphoreType.DMA((10, max(n_obs, n_cam))),
        ],
        compiler_params=pltpu.CompilerParams(
            collective_id=0, has_side_effects=True, vmem_limit_bytes=48 * 1024 * 1024
        ),
    )(cameras, points, measured, sqrt_weight, cam_index, point_slot, block_owner, valid_count)


def solution(mesh):
    return jax.shard_map(
        local,
        mesh=mesh,
        in_specs=(
            P(None, ("groups", "cam")),
            P(None, ("groups", "obs")),
            P(("groups", "obs", "cam"), None, None),
            P(("groups", "obs", "cam"), None),
            P(("groups", "obs", "cam"), None),
            P(("groups", "obs", "cam"), None),
            P(("groups", "obs", "cam"), None),
            P(("groups", "obs", "cam")),
        ),
        out_specs=(P(None, ("groups", "cam")), P(None, ("groups", "obs"))),
        check_vma=False,
    )
```

time: 1290 us -> 87.7 us (0.07)
  other arithmetic: 508 us -> 0 us
  blocking collectives: 381 us -> 0 us
  local copies, waits for them, and re-layouts: 385 us -> 5.4 us
  Pallas kernels: 0 us -> 81.2 us
    scatter-add x66 -> x0, other arithmetic: 504 us -> none  [the longest x45 344 us: camera_sum(): jnp.zeros((cams_all,), jnp.float32).at[flat_cam].add(summand.reshape(-1))]
    gather x60 -> x0, local copies, waits for them, and re-layouts: 377 us -> none  [the longest x36 247 us: along_cameras(): at_obs = [full_dir[member][cam_index] for member in range(9)]]
    all_gather x20 -> x0, blocking collectives: 158 us -> none  [the longest x15 132 us: at_points(): gathered = lax.all_gather(tuple(point_values), 'obs', axis=0, tiled=True)]
    unnamed x9 -> x0, blocking collectives: 123 us -> none
    psum x14 -> x0, blocking collectives: 101 us -> none  [the longest x4 39.2 us: camera_sum(): return lax.psum(shares, 'obs')]
    pallas_call x0 -> x1, Pallas kernels: none -> 81.2 us  [local(): pl.pallas_call(functools.partial(kernel, n_obs, n_cam), out_shape=(jax.Sh...]
where the time goes in v1:
time: 87.7 us; the launch traced here: 87.3 us
  Pallas kernels  81.2 us (93%)
  local copies, waits for them, and re-layouts  5.4 us (6%)
    pallas_call x1, Pallas kernels, local(): pl.pallas_call(functools.partial(kernel, n_obs, n_cam), out_shape=(jax.Sh...  81.2 us
    unnamed x17, local copies, waits for them, and re-layouts  5.4 us

profile of v1, /device:TPU:0, one launch (start us, length us, event | category | flops | bytes accessed | tf_op | source)
XLA Modules:
  0.0 87.3 jit_solution(4492719428413008408)
XLA Ops:
  0.6 0.0 copy-start.6
  0.6 0.0 copy-start.2
  0.7 0.7 copy.10.owner
  1.4 0.0 copy-done.6
  1.4 0.0 copy-done.2
  1.4 0.0 copy-start
  1.4 0.7 copy-done
  2.1 0.0 copy-start.1
  2.1 0.7 copy-done.1
  2.8 0.0 copy-start.3
  2.8 0.7 copy-done.3
  3.5 0.0 copy-start.4
  3.5 0.7 copy-done.4
  4.2 0.0 copy-start.5
  4.2 0.7 copy-done.5
  4.9 81.2 %shard_map.95 = (f32[9,128]{1,0:T(8,128)S(1)}, f32[3,256]{1,0:T(4,128)S(1)}) custom-call(f32[9,128]{1,0:T(8,128)S(1)} %copy-done, f32[3,256]{1,0:T(4,128)S(1)} %copy-done.2, f32[8,2,128]{2,1,0:T(2,128)S(1)} %copy-done.1, f32[8,128]{1,0:T(8,128)S(1)} %copy-done.3, s32[8,128]{1,0:T(8,128)S(1)} %copy-done.4, s32[8,128]{1,0:T(8,128)S(1)} %copy-done.5, ...), custom_call_target="tpu_custom_call" | custom-call | tf_op jit(solution)/shard_map/pallas_call | solution.py:307
  86.1 0.6 copy.13
  86.7 0.6 copy.14
Async XLA Ops:
  0.6 0.8 copy-start.6
  0.6 0.8 copy-start.2
  1.4 0.7 copy-start
  2.1 0.7 copy-start.1
  2.8 0.7 copy-start.3
  3.5 0.7 copy-start.4
  4.2 0.7 copy-start.5

commit v2 on v1

--- a/solution.py
+++ b/solution.py
@@ -266,7 +266,7 @@
         return jnp.sum(jnp.sum(a * b, axis=0, keepdims=True), axis=1, keepdims=True)
 
     def iterate(_, state):
-        x, res, direction, rz = state
+        x, res, direction, rz, *sums = state
         along_u, along_v, pushed = push(direction)
         pulled_u, pulled_v = at_slots(solve(pushed))
         left_u, left_v = along_u - pulled_u, along_v - pulled_v
@@ -274,18 +274,19 @@
         image = unpack(all_sum(sum_c, sum_o, 8), 0) + DAMPING * direction
         alpha = rz / dot(direction, image)
         x = x + alpha * direction
+        sums = [sums[i] + alpha * pushed[i] for i in range(3)]
         res = res - alpha * image
         pre = res / precond
         rz_new = dot(res, pre)
-        return x, res, pre + (rz_new / rz) * direction, rz_new
+        return (x, res, pre + (rz_new / rz) * direction, rz_new, *sums)
 
     pre = rhs / precond
-    state = (jnp.zeros_like(rhs), rhs, pre, dot(rhs, pre))
-    x = lax.fori_loop(0, ITERS, iterate, state)[0]
+    sums = [jnp.zeros_like(gradient[0])] * 3
+    state = (jnp.zeros_like(rhs), rhs, pre, dot(rhs, pre), *sums)
+    x, _, _, _, *pushed = lax.fori_loop(0, ITERS, iterate, state)
     full_x[...] = x
     at = pl.multiple_of(me["cam"] * cams_local, cams_local)
     cam_out[...] = full_x[0:9, pl.ds(at, cams_local)]
-    pushed = push(x)[2]
     steps = solve([-(gradient[i] + pushed[i]) for i in range(3)])
     for i in range(3):
         full_p[i] = steps[i]

time: 87.7 us -> 79.4 us (0.905)
  Pallas kernels: 81.2 us -> 73 us
    pallas_call x1, Pallas kernels: 81.2 us -> 73 us  [local(): pl.pallas_call(functools.partial(kernel, n_obs, n_cam), out_shape=(jax.Sh...]
where the time goes in v2:
time: 79.4 us; the launch traced here: 79 us
  Pallas kernels  73 us (92%)
  local copies, waits for them, and re-layouts  5.4 us (7%)
    pallas_call x1, Pallas kernels, local(): pl.pallas_call(functools.partial(kernel, n_obs, n_cam), out_shape=(jax.Sh...  73 us
    unnamed x17, local copies, waits for them, and re-layouts  5.4 us

profile of v2, /device:TPU:0, one launch (start us, length us, event | category | flops | bytes accessed | tf_op | source)
XLA Modules:
  0.0 79.0 jit_solution(5296339261861259408)
XLA Ops:
  0.6 0.0 copy-start.6
  0.6 0.0 copy-start.2
  0.7 0.7 copy.10.owner
  1.4 0.0 copy-done.6
  1.4 0.0 copy-done.2
  1.4 0.0 copy-start
  1.4 0.7 copy-done
  2.1 0.0 copy-start.1
  2.1 0.7 copy-done.1
  2.8 0.0 copy-start.3
  2.8 0.7 copy-done.3
  3.5 0.0 copy-start.4
  3.5 0.7 copy-done.4
  4.2 0.0 copy-start.5
  4.2 0.7 copy-done.5
  4.9 73.0 %shard_map.95 = (f32[9,128]{1,0:T(8,128)S(1)}, f32[3,256]{1,0:T(4,128)S(1)}) custom-call(f32[9,128]{1,0:T(8,128)S(1)} %copy-done, f32[3,256]{1,0:T(4,128)S(1)} %copy-done.2, f32[8,2,128]{2,1,0:T(2,128)S(1)} %copy-done.1, f32[8,128]{1,0:T(8,128)S(1)} %copy-done.3, s32[8,128]{1,0:T(8,128)S(1)} %copy-done.4, s32[8,128]{1,0:T(8,128)S(1)} %copy-done.5, ...), custom_call_target="tpu_custom_call" | custom-call | tf_op jit(solution)/shard_map/pallas_call | solution.py:308
  77.9 0.6 copy.13
  78.5 0.6 copy.14
Async XLA Ops:
  0.6 0.8 copy-start.6
  0.6 0.8 copy-start.2
  1.4 0.7 copy-start
  2.1 0.7 copy-start.1
  2.8 0.7 copy-start.3
  3.5 0.7 copy-start.4
  4.2 0.7 copy-start.5

commit v3 on v2

--- a/solution.py
+++ b/solution.py
@@ -81,11 +81,11 @@
 
 def kernel(
     n_obs, n_cam,
-    cameras, points, measured, weights, cam_index, point_slot, owner, valid,
+    cameras_in, points_in, measured_in, weights_in, cam_index_in, point_slot_in, owner, valid,
     cam_out, point_out,
     cams_in, pts_in, setup_c, setup_o, pre_c, pre_o, push_c, push_o, sum_c, sum_o,
     cam_hot, pt_hot, slopes_u, slopes_v, full_x, full_p,
-    send, recv,
+    send, recv, load, cameras, points, measured, weights, cam_index, point_slot,
 ):
     blocks, width = cam_index.shape
     slots = blocks * width
@@ -100,6 +100,11 @@
     def partner(axis, step):
         return {axis: lax.rem(me[axis] + step, size[axis])}
 
+    sources = (cameras_in, points_in, measured_in, weights_in, cam_index_in, point_slot_in)
+    targets = (cameras, points, measured, weights, cam_index, point_slot)
+    loads = [pltpu.make_async_copy(a, b, load.at[i]) for i, (a, b) in enumerate(zip(sources, targets))]
+    for copy in loads:
+        copy.start()
     barrier = pltpu.get_barrier_semaphore()
     for axis in ("cam", "obs"):
         for step in range(1, size[axis]):
@@ -107,6 +112,8 @@
                 barrier, inc=1, device_id=partner(axis, step), device_id_type=pl.DeviceIdType.MESH
             )
     pl.semaphore_wait(barrier, n_obs + n_cam - 2)
+    for copy in loads:
+        copy.wait()
 
     def begin(buf, number, axis):
         copies = []
@@ -148,7 +155,7 @@
 
     cam_line = line([cam_index[b : b + 1, :] for b in range(blocks)])
     slot_line = line([point_slot[b : b + 1, :] for b in range(blocks)])
-    owner_line = line([jnp.full((1, width), owner[b, 0], jnp.int32) for b in range(blocks)])
+    owner_line = line([jnp.broadcast_to(owner[b : b + 1, 0:1], (1, width)) for b in range(blocks)])
     meas_u = line([measured[b, 0:1, :] for b in range(blocks)])
     meas_v = line([measured[b, 1:2, :] for b in range(blocks)])
     lanes = lax.broadcasted_iota(jnp.int32, (1, width), 1)
@@ -219,7 +226,7 @@
 
     rows = [land_u[i] * land_u[j] + land_v[i] * land_v[j] for i, j in PAIR_LIST]
     rows += [land_u[i] * resid_u + land_v[i] * resid_v for i in range(3)]
-    setup_c[me["cam"]] = to_points(rows)
+    setup_c[me["cam"]] = to_points(rows)[: setup_c.shape[1]]
     totals = members_of(all_sum(setup_c, setup_o, 2), 9)
     full = [totals[i] + DAMPING if i in (0, 3, 5) else totals[i] for i in range(6)]
     gradient = totals[6:]
@@ -299,19 +306,20 @@
     pts_local, cams_local = points.shape[1], cameras.shape[1]
     cams_all = cams_local * n_cam
     one = ceil_to(9 * (cams_all // 128), 8)
-    three, nine = ceil_to(3 * n_obs, 16), ceil_to(9 * n_obs, 16)
+    three, nine = ceil_to(3 * n_obs, 16), ceil_to(9 * n_obs, 8)
 
     def pair(rows, columns):
         return [pltpu.VMEM((count, rows, columns), F32) for count in (n_cam, n_obs)]
 
     vmem, smem = pl.BlockSpec(memory_space=pltpu.VMEM), pl.BlockSpec(memory_space=pltpu.SMEM)
+    loaded = (cameras, points, measured, sqrt_weight, cam_index, point_slot)
     return pl.pallas_call(
         functools.partial(kernel, n_obs, n_cam),
         out_shape=(
             jax.ShapeDtypeStruct((9, cams_local), F32),
             jax.ShapeDtypeStruct((3, pts_local), F32),
         ),
-        in_specs=[vmem] * 6 + [smem] * 2,
+        in_specs=[pl.BlockSpec(memory_space=pl.ANY)] * 6 + [vmem, smem],
         out_specs=(vmem, vmem),
         scratch_shapes=[
             pltpu.VMEM((n_cam, 16, cams_local), F32),
@@ -328,6 +336,8 @@
             pltpu.VMEM((3, n_obs, pts_local), F32),
             pltpu.SemaphoreType.DMA((10, max(n_obs, n_cam))),
             pltpu.SemaphoreType.DMA((10, max(n_obs, n_cam))),
+            pltpu.SemaphoreType.DMA((6,)),
+            *[pltpu.VMEM(x.shape, x.dtype) for x in loaded],
         ],
         compiler_params=pltpu.CompilerParams(
             collective_id=0, has_side_effects=True, vmem_limit_bytes=48 * 1024 * 1024

time: 79.4 us -> 78.6 us (0.990)
  Pallas kernels: 73 us -> 72.1 us
    pallas_call x1, Pallas kernels: 73 us -> 72.1 us  [local(): pl.pallas_call(functools.partial(kernel, n_obs, n_cam), out_shape=(jax.Sh...]
where the time goes in v3:
time: 78.6 us; the launch traced here: 78.2 us
  Pallas kernels  72.1 us (92%)
  local copies, waits for them, and re-layouts  5.4 us (7%)
    pallas_call x1, Pallas kernels, local(): pl.pallas_call(functools.partial(kernel, n_obs, n_cam), out_shape=(jax.Sh...  72.1 us
    unnamed x17, local copies, waits for them, and re-layouts  5.4 us

profile of v3, /device:TPU:0, one launch (start us, length us, event | category | flops | bytes accessed | tf_op | source)
XLA Modules:
  0.0 78.2 jit_solution(3012902033870825759)
XLA Ops:
  0.6 0.0 copy-start.6
  0.6 0.0 copy-start.2
  0.7 0.7 copy.10.owner
  1.4 0.0 copy-done.6
  1.4 0.0 copy-done.2
  1.4 0.0 copy-start
  1.4 0.7 copy-done
  2.1 0.0 copy-start.1
  2.1 0.7 copy-done.1
  2.8 0.0 copy-start.3
  2.8 0.7 copy-done.3
  3.5 0.0 copy-start.4
  3.5 0.7 copy-done.4
  4.2 0.0 copy-start.5
  4.2 0.7 copy-done.5
  4.9 72.1 %shard_map.95 = (f32[9,128]{1,0:T(8,128)S(1)}, f32[3,256]{1,0:T(4,128)S(1)}) custom-call(f32[9,128]{1,0:T(8,128)S(1)} %copy-done, f32[3,256]{1,0:T(4,128)S(1)} %copy-done.2, f32[8,2,128]{2,1,0:T(2,128)S(1)} %copy-done.1, f32[8,128]{1,0:T(8,128)S(1)} %copy-done.3, s32[8,128]{1,0:T(8,128)S(1)} %copy-done.4, s32[8,128]{1,0:T(8,128)S(1)} %copy-done.5, ...), custom_call_target="tpu_custom_call" | custom-call | tf_op jit(solution)/shard_map/pallas_call | solution.py:316
  77.0 0.6 copy.13
  77.6 0.6 copy.14
Async XLA Ops:
  0.6 0.8 copy-start.6
  0.6 0.8 copy-start.2
  1.4 0.7 copy-start
  2.1 0.7 copy-start.1
  2.8 0.7 copy-start.3
  3.5 0.7 copy-start.4
  4.2 0.7 copy-start.5

commit v4 on v3

--- a/solution.py
+++ b/solution.py
@@ -15,6 +15,10 @@
 
 def ceil_to(number, step):
     return -(-number // step) * step
+
+
+def by_chips(n_obs, n_cam):
+    return n_cam % 2 == 0 and n_obs * n_cam <= 16
 
 
 def cross(a, b):
@@ -83,7 +87,7 @@
     n_obs, n_cam,
     cameras_in, points_in, measured_in, weights_in, cam_index_in, point_slot_in, owner, valid,
     cam_out, point_out,
-    cams_in, pts_in, setup_c, setup_o, pre_c, pre_o, push_c, push_o, sum_c, sum_o,
+    cams_in, pts_in, setup_c, setup_o, setup_p, pre_c, pre_o, pre_p, push_c, push_o, push_p, sum_c, sum_o, sum_p,
     cam_hot, pt_hot, slopes_u, slopes_v, full_x, full_p,
     send, recv, load, cameras, points, measured, weights, cam_index, point_slot,
 ):
@@ -97,8 +101,24 @@
     me = {"obs": lax.axis_index("obs"), "cam": lax.axis_index("cam")}
     size = {"obs": n_obs, "cam": n_cam}
 
+    flat, half = by_chips(n_obs, n_cam), n_cam // 2
+    parity = lax.rem(me["cam"], 2)
+    if flat:
+        me.update(pair=parity, chips=me["obs"] * half + me["cam"] // 2)
+        me.update(every=me["obs"] * n_cam + me["cam"])
+        size.update(pair=2, chips=n_obs * half, every=n_obs * n_cam)
+    lead = "pair" if flat else "cam"
+    greeted = ("every",) if flat else ("cam", "obs")
+
     def partner(axis, step):
-        return {axis: lax.rem(me[axis] + step, size[axis])}
+        other = lax.rem(me[axis] + step, size[axis])
+        if axis == "pair":
+            return {"cam": me["cam"] // 2 * 2 + other}
+        if axis == "chips":
+            return {"obs": other // half, "cam": lax.rem(other, half) * 2 + parity}
+        if axis == "every":
+            return {"obs": other // n_cam, "cam": lax.rem(other, n_cam)}
+        return {axis: other}
 
     sources = (cameras_in, points_in, measured_in, weights_in, cam_index_in, point_slot_in)
     targets = (cameras, points, measured, weights, cam_index, point_slot)
@@ -106,21 +126,22 @@
     for copy in loads:
         copy.start()
     barrier = pltpu.get_barrier_semaphore()
-    for axis in ("cam", "obs"):
+    for axis in greeted:
         for step in range(1, size[axis]):
             pl.semaphore_signal(
                 barrier, inc=1, device_id=partner(axis, step), device_id_type=pl.DeviceIdType.MESH
             )
-    pl.semaphore_wait(barrier, n_obs + n_cam - 2)
+    pl.semaphore_wait(barrier, sum(size[axis] - 1 for axis in greeted))
     for copy in loads:
         copy.wait()
 
-    def begin(buf, number, axis):
+    def begin(buf, number, axis, rows=None):
+        own = buf.at[me[axis]] if rows is None else buf.at[me[axis], rows]
         copies = []
         for step in range(1, size[axis]):
             copy = pltpu.make_async_remote_copy(
-                src_ref=buf.at[me[axis]],
-                dst_ref=buf.at[me[axis]],
+                src_ref=own,
+                dst_ref=own,
                 send_sem=send.at[number, step],
                 recv_sem=recv.at[number, step],
                 device_id=partner(axis, step),
@@ -140,7 +161,17 @@
             out = out + buf[i]
         return out
 
-    def all_sum(first, second, number):
+    def all_sum(first, second, third, number):
+        if flat:
+            rows = second.shape[1]
+            mine = pl.ds(pl.multiple_of(parity * rows, 8), rows)
+            theirs = pl.ds(pl.multiple_of((1 - parity) * rows, 8), rows)
+            finish(begin(first, number, "pair", theirs))
+            second[me["chips"]] = first[0, mine, :] + first[1, mine, :]
+            finish(begin(second, number + 1, "chips"))
+            third[parity] = total(second, size["chips"])
+            finish(begin(third, number + 2, "pair"))
+            return jnp.concatenate([third[0], third[1]], axis=0)
         finish(begin(first, number, "cam"))
         second[me["obs"]] = total(first, n_cam)
         finish(begin(second, number + 1, "obs"))
@@ -196,9 +227,9 @@
         for q, x in enumerate(vectors):
             for j in range(chunks):
                 at, part = q * one + 8 * j, slice(128 * j, 128 * j + 128)
-                buf[me["cam"], at : at + 8, :] = x[0:8, part]
+                buf[me[lead], at : at + 8, :] = x[0:8, part]
                 at = q * one + 8 * chunks + j
-                buf[me["cam"], at : at + 1, :] = x[8:9, part]
+                buf[me[lead], at : at + 1, :] = x[8:9, part]
 
     def unpack(table, q):
         base = q * one
@@ -207,8 +238,8 @@
         last = line([table[base + j : base + j + 1] for j in range(chunks)])
         return jnp.concatenate([top, last, jnp.zeros((7, cams_all), F32)], axis=0)
 
-    pre_c[me["cam"]] = jnp.zeros(pre_c.shape[1:], F32)
-    sum_c[me["cam"]] = jnp.zeros(sum_c.shape[1:], F32)
+    pre_c[me[lead]] = jnp.zeros(pre_c.shape[1:], F32)
+    sum_c[me[lead]] = jnp.zeros(sum_c.shape[1:], F32)
     finish(copies)
 
     params = gather(line([cams_in[j] for j in range(n_cam)]), cam_hot)
@@ -226,8 +257,8 @@
 
     rows = [land_u[i] * land_u[j] + land_v[i] * land_v[j] for i, j in PAIR_LIST]
     rows += [land_u[i] * resid_u + land_v[i] * resid_v for i in range(3)]
-    setup_c[me["cam"]] = to_points(rows)[: setup_c.shape[1]]
-    totals = members_of(all_sum(setup_c, setup_o, 2), 9)
+    setup_c[me[lead]] = to_points(rows)[: setup_c.shape[1]]
+    totals = members_of(all_sum(setup_c, setup_o, setup_p, 2), 9)
     full = [totals[i] + DAMPING if i in (0, 3, 5) else totals[i] for i in range(6)]
     gradient = totals[6:]
     minors = (
@@ -258,7 +289,7 @@
         cam_hot,
     )
     pack(pre_c, [both[:16], both[16:]])
-    table = all_sum(pre_c, pre_o, 4)
+    table = all_sum(pre_c, pre_o, pre_p, 5)
     rhs = unpack(table, 0)
     precond = unpack(table, 1) + DAMPING
 
@@ -266,8 +297,8 @@
         at_obs = gather(x, cam_hot)
         along_u = jnp.sum(slopes_u[...] * at_obs, axis=0, keepdims=True)
         along_v = jnp.sum(slopes_v[...] * at_obs, axis=0, keepdims=True)
-        push_c[me["cam"]] = to_points([land_u[i] * along_u + land_v[i] * along_v for i in range(3)])
-        return along_u, along_v, members_of(all_sum(push_c, push_o, 6), 3)
+        push_c[me[lead]] = to_points([land_u[i] * along_u + land_v[i] * along_v for i in range(3)])
+        return along_u, along_v, members_of(all_sum(push_c, push_o, push_p, 8), 3)
 
     def dot(a, b):
         return jnp.sum(jnp.sum(a * b, axis=0, keepdims=True), axis=1, keepdims=True)
@@ -278,7 +309,7 @@
         pulled_u, pulled_v = at_slots(solve(pushed))
         left_u, left_v = along_u - pulled_u, along_v - pulled_v
         pack(sum_c, [scatter(slopes_u[...] * left_u + slopes_v[...] * left_v, cam_hot)])
-        image = unpack(all_sum(sum_c, sum_o, 8), 0) + DAMPING * direction
+        image = unpack(all_sum(sum_c, sum_o, sum_p, 11), 0) + DAMPING * direction
         alpha = rz / dot(direction, image)
         x = x + alpha * direction
         sums = [sums[i] + alpha * pushed[i] for i in range(3)]
@@ -306,10 +337,21 @@
     pts_local, cams_local = points.shape[1], cameras.shape[1]
     cams_all = cams_local * n_cam
     one = ceil_to(9 * (cams_all // 128), 8)
-    three, nine = ceil_to(3 * n_obs, 16), ceil_to(9 * n_obs, 8)
+    three, nine = ceil_to(3 * n_obs, 16), ceil_to(9 * n_obs, 16)
+
+    flat, chips = by_chips(n_obs, n_cam), n_obs * n_cam // 2
 
     def pair(rows, columns):
-        return [pltpu.VMEM((count, rows, columns), F32) for count in (n_cam, n_obs)]
+        if not flat:
+            return [pltpu.VMEM((n, rows, columns), F32) for n in (n_cam, n_obs)] + [
+                pltpu.VMEM((1, 8, 128), F32)
+            ]
+        part = rows // 2
+        return [
+            pltpu.VMEM((2, rows, columns), F32),
+            pltpu.VMEM((chips, part, columns), F32),
+            pltpu.VMEM((2, part, columns), F32),
+        ]
 
     vmem, smem = pl.BlockSpec(memory_space=pltpu.VMEM), pl.BlockSpec(memory_space=pltpu.SMEM)
     loaded = (cameras, points, measured, sqrt_weight, cam_index, point_slot)
@@ -327,15 +369,15 @@
             *pair(nine, pts_local),
             *pair(2 * one, 128),
             *pair(three, pts_local),
-            *pair(one, 128),
+            *pair(ceil_to(one, 16), 128),
             pltpu.VMEM((cams_all, slots), BF16),
             pltpu.VMEM((pts_local, slots), BF16),
             pltpu.VMEM((16, slots), F32),
             pltpu.VMEM((16, slots), F32),
             pltpu.VMEM((16, cams_all), F32),
             pltpu.VMEM((3, n_obs, pts_local), F32),
-            pltpu.SemaphoreType.DMA((10, max(n_obs, n_cam))),
-            pltpu.SemaphoreType.DMA((10, max(n_obs, n_cam))),
+            pltpu.SemaphoreType.DMA((14, max(n_obs, n_cam, chips if flat else 0))),
+            pltpu.SemaphoreType.DMA((14, max(n_obs, n_cam, chips if flat else 0))),
             pltpu.SemaphoreType.DMA((6,)),
             *[pltpu.VMEM(x.shape, x.dtype) for x in loaded],
         ],

time: 78.6 us -> 77.5 us (0.986)
  Pallas kernels: 72.1 us -> 71 us
    pallas_call x1, Pallas kernels: 72.1 us -> 71 us  [local(): pl.pallas_call(functools.partial(kernel, n_obs, n_cam), out_shape=(jax.Sh...]
where the time goes in v4:
time: 77.5 us; the launch traced here: 77.1 us
  Pallas kernels  71 us (92%)
  local copies, waits for them, and re-layouts  5.4 us (7%)
    pallas_call x1, Pallas kernels, local(): pl.pallas_call(functools.partial(kernel, n_obs, n_cam), out_shape=(jax.Sh...  71 us
    unnamed x17, local copies, waits for them, and re-layouts  5.4 us

profile of v4, /device:TPU:0, one launch (start us, length us, event | category | flops | bytes accessed | tf_op | source)
XLA Modules:
  0.0 77.1 jit_solution(11929385411637744263)
XLA Ops:
  0.6 0.0 copy-start.6
  0.6 0.0 copy-start.2
  0.7 0.7 copy.10.owner
  1.4 0.0 copy-done.6
  1.4 0.0 copy-done.2
  1.4 0.0 copy-start
  1.4 0.7 copy-done
  2.1 0.0 copy-start.1
  2.1 0.7 copy-done.1
  2.8 0.0 copy-start.3
  2.8 0.7 copy-done.3
  3.5 0.0 copy-start.4
  3.5 0.7 copy-done.4
  4.2 0.0 copy-start.5
  4.2 0.7 copy-done.5
  4.9 71.0 %shard_map.95 = (f32[9,128]{1,0:T(8,128)S(1)}, f32[3,256]{1,0:T(4,128)S(1)}) custom-call(f32[9,128]{1,0:T(8,128)S(1)} %copy-done, f32[3,256]{1,0:T(4,128)S(1)} %copy-done.2, f32[8,2,128]{2,1,0:T(2,128)S(1)} %copy-done.1, f32[8,128]{1,0:T(8,128)S(1)} %copy-done.3, s32[8,128]{1,0:T(8,128)S(1)} %copy-done.4, s32[8,128]{1,0:T(8,128)S(1)} %copy-done.5, ...), custom_call_target="tpu_custom_call" | custom-call | tf_op jit(solution)/shard_map/pallas_call | solution.py:358
  75.9 0.6 copy.13
  76.5 0.6 copy.14
Async XLA Ops:
  0.6 0.8 copy-start.6
  0.6 0.8 copy-start.2
  1.4 0.7 copy-start
  2.1 0.7 copy-start.1
  2.8 0.7 copy-start.3
  3.5 0.7 copy-start.4
  4.2 0.7 copy-start.5

commit v5 on v4

--- a/solution.py
+++ b/solution.py
@@ -151,9 +151,16 @@
             copies.append(copy)
         return copies
 
+    sending = []
+
+    def sent():
+        while sending:
+            sending.pop().wait_send()
+
     def finish(copies):
         for copy in copies:
-            copy.wait()
+            copy.wait_recv()
+        sending.extend(copies)
 
     def total(buf, count):
         out = buf[0]
@@ -170,7 +177,9 @@
             second[me["chips"]] = first[0, mine, :] + first[1, mine, :]
             finish(begin(second, number + 1, "chips"))
             third[parity] = total(second, size["chips"])
-            finish(begin(third, number + 2, "pair"))
+            copies = begin(third, number + 2, "pair")
+            sent()
+            finish(copies)
             return jnp.concatenate([third[0], third[1]], axis=0)
         finish(begin(first, number, "cam"))
         second[me["obs"]] = total(first, n_cam)
@@ -316,8 +325,10 @@
         res = res - alpha * image
         pre = res / precond
         rz_new = dot(res, pre)
+        sent()
         return (x, res, pre + (rz_new / rz) * direction, rz_new, *sums)
 
+    sent()
     pre = rhs / precond
     sums = [jnp.zeros_like(gradient[0])] * 3
     state = (jnp.zeros_like(rhs), rhs, pre, dot(rhs, pre), *sums)

time: 77.5 us -> 75.5 us (0.974)
  Pallas kernels: 71 us -> 69 us
    pallas_call x1, Pallas kernels: 71 us -> 69 us  [local(): pl.pallas_call(functools.partial(kernel, n_obs, n_cam), out_shape=(jax.Sh...]
where the time goes in v5:
time: 75.5 us; the launch traced here: 75 us
  Pallas kernels  69 us (91%)
  local copies, waits for them, and re-layouts  5.4 us (7%)
    pallas_call x1, Pallas kernels, local(): pl.pallas_call(functools.partial(kernel, n_obs, n_cam), out_shape=(jax.Sh...  69 us
    unnamed x17, local copies, waits for them, and re-layouts  5.4 us

profile of v5, /device:TPU:0, one launch (start us, length us, event | category | flops | bytes accessed | tf_op | source)
XLA Modules:
  0.0 75.0 jit_solution(14797115815744296054)
XLA Ops:
  0.6 0.0 copy-start.6
  0.6 0.0 copy-start.2
  0.7 0.7 copy.10.owner
  1.4 0.0 copy-done.6
  1.4 0.0 copy-done.2
  1.4 0.0 copy-start
  1.4 0.7 copy-done
  2.1 0.0 copy-start.1
  2.1 0.7 copy-done.1
  2.8 0.0 copy-start.3
  2.8 0.7 copy-done.3
  3.5 0.0 copy-start.4
  3.5 0.7 copy-done.4
  4.2 0.0 copy-start.5
  4.2 0.7 copy-done.5
  4.9 69.0 %shard_map.95 = (f32[9,128]{1,0:T(8,128)S(1)}, f32[3,256]{1,0:T(4,128)S(1)}) custom-call(f32[9,128]{1,0:T(8,128)S(1)} %copy-done, f32[3,256]{1,0:T(4,128)S(1)} %copy-done.2, f32[8,2,128]{2,1,0:T(2,128)S(1)} %copy-done.1, f32[8,128]{1,0:T(8,128)S(1)} %copy-done.3, s32[8,128]{1,0:T(8,128)S(1)} %copy-done.4, s32[8,128]{1,0:T(8,128)S(1)} %copy-done.5, ...), custom_call_target="tpu_custom_call" | custom-call | tf_op jit(solution)/shard_map/pallas_call | solution.py:369
  73.8 0.6 copy.13
  74.4 0.6 copy.14
Async XLA Ops:
  0.6 0.8 %copy-start.6 = (s32[8]{0:T(128)S(1)}, s32[8]{0:T(128)}, u32[]{:S(2)}) copy-start(s32[8]{0:T(128)} %valid.1) | copy-start | bytes 100
  0.6 0.8 %copy-start.2 = (f32[3,256]{1,0:T(4,128)S(1)}, f32[3,256]{1,0:T(4,128)}, u32[]{:S(2)}) copy-start(f32[3,256]{1,0:T(4,128)} %points_in.1) | copy-start | bytes 9220
  1.4 0.7 copy-start
  2.1 0.7 copy-start.1
  2.8 0.7 copy-start.3
  3.5 0.7 copy-start.4
  4.2 0.7 copy-start.5
